TPU v7x, 32 devices: a whole 2x2x4 slice. The times are simulated.
32 devices in a mesh: row: 4 (over y, x), col: 8 (over z, core).
Axes of the slice: x: 2, y: 2, z: 4, core: 2. Of those that a mesh axis runs over, the one named last changes fastest.
Arguments:
- vectors: bfloat16 [16, 16384], P(None, ('row', 'col')), may hold values from -6 to 6
- blocks: bfloat16 [4, 1536, 128, 128], P('row', 'col'), may hold values from -0.09375 to 0.09375
- row_ptr: int32 [4, 264], P('row', 'col'), may hold values from 0 to 192, as said below
- col_idx: int32 [4, 1536], P('row', 'col'), may hold values from 0 to 15, as said below
Outputs:
- product: float32 [16, 16384], P(None, ('row', 'col'))
Inputs may be any that keep to these rules, and one draw needn't show every extreme that they name: For each tile, row_ptr starts at 0, never falls, and ends at the tile's count of live slots; at least one tile has exactly 192 live slots in every draw, and counts differ strongly from tile to tile. `col_idx`: within each block row of a tile the live slots name strictly rising block columns, so no block position of a tile is stored twice; slots at or past a tile's count hold a valid column and are unused.
All inputs are finite; a program needn't handle non-finite values.
Results may differ from a plain program's by a relative error of at most 0.0003.
Values may be sent and summed in bfloat16 or wider, within the bound.
A program may use at most 64 MiB of HBM per device.

v0:
```python
import jax
import jax.numpy as jnp
from jax import lax
from jax.sharding import PartitionSpec as P


def tile_terms(row_side, col_side, tile_blocks, pointers, columns):
    slot_ids = jnp.arange(tile_blocks.shape[0], dtype=jnp.int32)
    live_slots = slot_ids < pointers[-1]
    slot_rows = jnp.sum((slot_ids[:, None] >= pointers[None, 1:]).astype(jnp.int32), axis=1)
    slot_rows = jnp.minimum(slot_rows, pointers.shape[0] - 2)
    count_vectors = row_side.shape[0]
    edge = tile_blocks.shape[1]
    row_blocks = row_side.reshape(count_vectors, -1, edge)
    col_blocks = col_side.reshape(count_vectors, -1, edge)
    picked_rows = jnp.take(row_blocks, slot_rows, axis=1)
    picked_cols = jnp.take(col_blocks, columns, axis=1)
    forward = jnp.einsum(
        "ksj,sij->ski", picked_cols, tile_blocks, preferred_element_type=jnp.float32
    )
    backward = jnp.einsum(
        "ksi,sij->skj", picked_rows, tile_blocks, preferred_element_type=jnp.float32
    )
    live_mask = live_slots[:, None, None]
    forward = jnp.where(live_mask, forward, jnp.zeros_like(forward))
    backward = jnp.where(live_mask, backward, jnp.zeros_like(backward))
    forward_sum = jax.ops.segment_sum(
        forward, slot_rows, num_segments=row_blocks.shape[1], indices_are_sorted=True
    )
    backward_sum = jax.ops.segment_sum(backward, columns, num_segments=col_blocks.shape[1])
    return (forward_sum, backward_sum)


def body(vectors, blocks, row_ptr, col_idx):
    count_vectors = vectors.shape[0]
    segment = vectors.shape[1]
    grid_rows = lax.axis_size("row")
    grid_cols = lax.axis_size("col")
    everything = lax.all_gather(vectors, ("row", "col"), axis=1, tiled=True)
    row_side = lax.dynamic_slice_in_dim(
        everything, lax.axis_index("row") * (grid_cols * segment), grid_cols * segment, 1
    )
    spread = everything.reshape(count_vectors, grid_rows, grid_cols, segment)
    col_side = lax.dynamic_slice_in_dim(spread, lax.axis_index("col"), 1, 2).reshape(
        count_vectors, grid_rows * segment
    )
    forward_sum, backward_sum = tile_terms(row_side, col_side, blocks[0], row_ptr[0], col_idx[0])
    forward_part = lax.psum_scatter(forward_sum, "col", scatter_dimension=0, tiled=True)
    backward_part = lax.psum_scatter(backward_sum, "row", scatter_dimension=0, tiled=True)
    combined = forward_part + backward_part
    return combined.transpose(1, 0, 2).reshape(count_vectors, segment)


def solution(mesh):
    in_specs = (
        P(None, ("row", "col")),
        P("row", "col", None, None),
        P("row", "col"),
        P("row", "col"),
    )
    out_specs = P(None, ("row", "col"))
    return jax.shard_map(body, mesh=mesh, in_specs=in_specs, out_specs=out_specs, check_vma=False)
```

profile of v0, /device:TPU:0, one launch (start us, length us, event | category | flops | bytes accessed | tf_op | source)
XLA Modules:
  0.0 129.6 jit_solution(4785380775646931471)
XLA Ops:
  6.5 0.0 reduce-scatter.5.cloned.1.call-start
  6.5 0.7 slice_bitcast_fusion
  7.3 0.1 convert_reduce_fusion
  7.4 1.2 slice.9
  8.6 45.5 %all_gather.3 = bf16[16,16384]{1,0:T(8,128)(2,1)S(1)} all-gather(bf16[16,512]{1,0:T(8,128)(2,1)} %param.4), channel_id=1, replica_groups=mesh['row'=4,'col'=8] {'row','col'}, dimensions={1}, use_global_device_ids=true | all-gather | bytes 540672 | tf_op jit(solution)/shard_map/all_gather | solution.py:39
  54.2 0.7 iota_compare_fusion.1
  54.9 0.8 gather_fusion.1
  55.7 0.0 copy-start.2
  55.7 4.2 %fusion.7 = f32[192,16,128]{2,1,0:T(8,128)S(1)} fusion(bf16[1,192,128,128]{3,2,1,0:T(8,128)(2,1)} %param.5, bf16[192,16,128]{2,1,0:T(8,128)(2,1)S(1)} %gather_fusion.1, pred[192]{0:T(512)(128)(4,1)S(1)} %compare_and_fusion, pred[192]{0:T(512)(128)(4,1)S(1)} %iota_compare_fusion.1), kind=kOutput, calls=%fused_computation.9 | convolution fusion | flops 101449728 | bytes 8651136 | tf_op jit(solution)/shard_map/ksi,sij->skj/dot_general | solution.py:21
  59.9 0.0 copy-done.2
  59.9 7.6 %scatter_fusion.1 = f32[16,16,128]{2,1,0:T(8,128)S(1)} fusion(f32[16,16,128]{2,1,0:T(8,128)S(1)} %broadcast_in_dim.43, s32[192]{0:T(256)S(1)} %bitcast.41, f32[192,16,128]{2,1,0:T(8,128)S(1)} %fusion.7), kind=kCustom, calls=%fused_computation.3 | custom fusion | flops 393216 | bytes 4719360 | tf_op jit(solution)/shard_map/scatter-add | solution.py:30
  67.6 0.6 copy-done
  68.2 0.0 reduce-scatter.5.cloned.1.call-update
  68.2 0.0 reduce-scatter.3.cloned.1.call-start
  68.3 0.2 copy.18
  68.5 0.4 dynamic-slice_reduce_fusion
  69.0 0.8 gather_fusion
  69.8 5.8 %fusion.4 = f32[192,16,128]{2,1,0:T(8,128)S(1)} fusion(bf16[1,192,128,128]{3,2,1,0:T(8,128)(2,1)} %param.5, bf16[192,16,128]{2,1,0:T(8,128)(2,1)S(1)} %gather_fusion, pred[192]{0:T(512)(128)(4,1)S(1)} %compare_and_fusion.1, pred[192]{0:T(512)(128)(4,1)S(1)} %iota_compare_fusion.1), kind=kOutput, calls=%fused_computation.8 | convolution fusion | flops 101449728 | bytes 8651136 | tf_op jit(solution)/shard_map/ksj,sij->ski/dot_general | solution.py:18
  75.7 8.0 %scatter_fusion = f32[32,16,128]{2,1,0:T(8,128)S(1)} fusion(f32[32,16,128]{2,1,0:T(8,128)S(1)} %broadcast_in_dim.39, s32[192]{0:T(256)S(1)} %broadcast_minimum_fusion, f32[192,16,128]{2,1,0:T(8,128)S(1)} %fusion.4), kind=kCustom, calls=%fused_computation.2 | custom fusion | flops 393216 | bytes 4719360 | tf_op jit(solution)/shard_map/scatter-add | solution.py:27
  83.6 0.7 copy-done.1
  84.3 0.0 reduce-scatter.3.cloned.1.call-update
  84.3 4.2 %reduce-scatter.5.cloned.1.call-done = f32[4,16,128]{2,1,0:T(8,128)} async-done(((f32[16,16,128]{2,1,0:T(8,128)}), f32[4,16,128]{2,1,0:T(8,128)}) %reduce-scatter.5.cloned.1.call-update) | async-done | bytes 32784 | tf_op jit(solution)/shard_map/reduce_scatter | solution.py:49
  88.5 32.8 %reduce-scatter.3.cloned.1.call-done = f32[4,16,128]{2,1,0:T(8,128)} async-done(((f32[32,16,128]{2,1,0:T(8,128)}), f32[4,16,128]{2,1,0:T(8,128)}) %reduce-scatter.3.cloned.1.call-update) | async-done | bytes 32784 | tf_op jit(solution)/shard_map/reduce_scatter | solution.py:48
  121.3 1.4 %copy_bitcast_fusion.1 = f32[16,512]{1,0:T(8,128)} fusion(f32[4,16,128]{2,1,0:T(8,128)} %reduce-scatter.3.cloned.1.call-done, f32[4,16,128]{2,1,0:T(8,128)} %reduce-scatter.5.cloned.1.call-done), kind=kLoop, calls=%fused_computation.21 | loop fusion | flops 8192 | bytes 98304 | tf_op jit(solution)/shard_map/reshape | solution.py:51
  (14 shorter events, 0.2 us)
Async XLA Ops:
  6.5 82.0 %reduce-scatter.5.cloned.1.call-start = ((), (), s32[]{:S(2)}) async-start(), calls=%async_computation.3 | async-start | bytes 163840 | tf_op jit(solution)/shard_map/reduce_scatter | solution.py:49
  55.7 4.3 %copy-start.2 = (s32[1,192]{1,0:T(1,128)S(1)}, s32[1,192]{1,0:T(1,128)}, u32[]{:S(2)}) copy-start(s32[1,192]{1,0:T(1,128)} %param.7) | copy-start | bytes 2308
  67.6 0.7 copy-start
  68.2 53.1 %reduce-scatter.3.cloned.1.call-start = ((), (), s32[]{:S(2)}) async-start(), calls=%async_computation.2 | async-start | bytes 294912 | tf_op jit(solution)/shard_map/reduce_scatter | solution.py:48
  83.6 0.7 copy-start.1
Sparse Core Ops, SparseCore 0:
  68.4 20.1 reduce-scatter.4
  90.9 30.4 reduce-scatter.2
where the time goes:
time: 130 us
  blocking collectives  45.5 us (35%)
  waiting for transfers between devices  37 us (28%)
  other arithmetic  17.8 us (14%)
  between operations  13.6 us (10%)
  matrix products  10.1 us (8%)
  local copies, waits for them, and re-layouts  5.57 us (4%)
    all_gather x1, blocking collectives, body(): everything = lax.all_gather(vectors, ('row', 'col'), axis=1, tiled=True)  45.5 us
    reduce_scatter x1, waiting for transfers between devices, body(): lax.psum_scatter(forward_sum, 'col', scatter_dimension=0, tiled=True)  32.8 us
    scatter-add x1, other arithmetic, tile_terms(): jax.ops.segment_sum(forward, slot_rows, num_segments=row_blocks.shape[1],...  7.97 us
    scatter-add x1, other arithmetic, tile_terms(): jax.ops.segment_sum(backward, columns, num_segments=col_blocks.shape[1])  7.61 us
    dot_general x1, matrix products, tile_terms(): jnp.einsum('ksj,sij->ski', picked_cols, tile_blocks, preferred_element_ty...  5.84 us
    dot_general x1, matrix products, tile_terms(): jnp.einsum('ksi,sij->skj', picked_rows, tile_blocks, preferred_element_ty...  4.23 us
    reduce_scatter x1, waiting for transfers between devices, body(): lax.psum_scatter(backward_sum, 'row', scatter_dimension=0, tiled=True)  4.2 us
  transfers between devices with their start and end apart: 2, of which 2 were waited for; matrix products, arithmetic and copies ran while one was open for 12% of the time, Pallas kernels for 0%

commit v1 on v0

v1 whole, which is shorter than its diff:
```python
import functools

import jax
import jax.numpy as jnp
from jax import lax
from jax.experimental import pallas as pl
from jax.experimental.pallas import tpu as pltpu
from jax.sharding import PartitionSpec as P

MESH = pl.DeviceIdType.MESH
GROUP = 16
FAR = 1 << 20


def slot_tables(pointers, columns, tile_cols):
    slots = columns.shape[1]
    tile_rows = pointers.shape[1] - 1
    i32 = jnp.int32

    def iota(shape, dim):
        return lax.broadcasted_iota(i32, shape, dim)

    def total(mask_or_value, axis):
        return jnp.sum(mask_or_value, axis=axis, keepdims=True)

    def count(mask, axis):
        return total(jnp.where(mask, 1, 0), axis)

    edge = (tile_rows + 1, tile_rows + 1)
    pointer_col = total(jnp.where(iota(edge, 0) == iota(edge, 1), pointers, 0), 1)
    wide = (tile_rows + 1, slots)
    rows = count(pointer_col <= iota(wide, 1), 0) - 1
    keep_row = jnp.where(count(pointer_col == iota(wide, 1), 0) == 0, 1, 0)

    square = (slots, slots)
    lane, sub = iota(square, 1), iota(square, 0)
    slot_row = iota((1, slots), 1)
    key = jnp.where(rows < tile_rows, columns * slots, FAR) + slot_row
    rows = jnp.minimum(rows, tile_rows - 1)
    same = lane == sub
    key_col = total(jnp.where(same, key, 0), 1)
    rows_col = total(jnp.where(same, rows, 0), 1)
    rank_col = count(key < key_col, 1)
    chosen = rank_col == lane
    order = total(jnp.where(chosen, sub, 0), 0)
    order_rows = total(jnp.where(chosen, rows_col, 0), 0)
    tall = (tile_cols, slots)
    ends_col = count(key < (iota(tall, 0) + 1) * slots, 1)
    starts = count(ends_col == iota(tall, 1), 0)
    keep_col = jnp.where((starts == 0) & (slot_row > 0), 1, 0)
    side = (tile_cols, tile_cols)
    ends = total(jnp.where(iota(side, 0) == iota(side, 1), ends_col, 0), 0)
    return keep_row, order, order_rows, keep_col, ends


def kernel(
    n_row, n_col, chunks,
    vec_hbm, blk_hbm, ptr_hbm, col_hbm, out_ref,
    vec, blk, ptr_s, col_s, ptr_v, col_v, table_v, table_s,
    row_side, col_side, run, fwd, bwd, near, fwd_in, bwd_in,
    vec_sem, blk_sem, idx_sem,
    rs_send, rs_recv, cs_send, cs_recv, near_send, near_recv,
    f_send, f_recv, b_send, b_recv,
):
    r = lax.axis_index("row")
    c = lax.axis_index("col")
    z, core = c // 2, c % 2
    nz = n_col // 2
    seg = vec.shape[1] // 128
    slots = blk.shape[0]
    per = slots // chunks
    f32 = jnp.float32

    get_vec = pltpu.make_async_copy(vec_hbm, vec, vec_sem)
    get_vec.start()
    index_copies = [
        pltpu.make_async_copy(src, dst, idx_sem.at[k])
        for k, (src, dst) in enumerate(
            ((ptr_hbm, ptr_v), (col_hbm, col_v), (ptr_hbm, ptr_s), (col_hbm, col_s))
        )
    ]
    for copy in index_copies:
        copy.start()

    def chunk_copy(k):
        part = pl.ds(k * per, per)
        return pltpu.make_async_copy(blk_hbm.at[0, part], blk.at[part], blk_sem.at[k])

    for k in range(chunks):
        chunk_copy(k).start()

    barrier = pltpu.get_barrier_semaphore()

    @pl.loop(1, n_row)
    def _(d):
        pl.semaphore_signal(barrier, inc=1, device_id=((r + d) % n_row, c), device_id_type=MESH)

    @pl.loop(1, n_col)
    def _(d):
        pl.semaphore_signal(barrier, inc=1, device_id=(r, (c + d) % n_col), device_id_type=MESH)

    get_vec.wait()
    for u in range(seg):
        piece = vec[:, u * 128:(u + 1) * 128]
        row_side[c * seg + u] = piece
        col_side[r * seg + u] = piece
    pl.semaphore_wait(barrier, n_row + n_col - 2)

    def cs_copy(d, mine):
        owner = r if mine else (r + n_row - d) % n_row
        part = pl.ds(owner * seg, seg)
        return pltpu.make_async_remote_copy(
            src_ref=col_side.at[part], dst_ref=col_side.at[part],
            send_sem=cs_send.at[d], recv_sem=cs_recv.at[d],
            device_id=((r + d) % n_row, c), device_id_type=MESH)

    def rs_copy(d, mine):
        owner = c if mine else (c + n_col - d) % n_col
        part = pl.ds(owner * seg, seg)
        return pltpu.make_async_remote_copy(
            src_ref=row_side.at[part], dst_ref=row_side.at[part],
            send_sem=rs_send.at[d], recv_sem=rs_recv.at[d],
            device_id=(r, (c + d) % n_col), device_id_type=MESH)

    @pl.loop(1, n_row)
    def _(d):
        cs_copy(d, True).start()

    @pl.loop(1, n_col)
    def _(d):
        rs_copy(d, True).start()

    for copy in index_copies:
        copy.wait()
    table_v[...] = jnp.zeros_like(table_v)
    tables = slot_tables(ptr_v[...], col_v[...], n_row * seg)
    for k, entry in enumerate(tables):
        table_v[k:k + 1, 0:entry.shape[1]] = entry
    put_table = pltpu.make_async_copy(table_v, table_s, idx_sem.at[0])
    put_table.start()
    run[slots] = jnp.zeros(run.shape[1:], f32)
    put_table.wait()

    @pl.loop(1, n_row)
    def _(d):
        cs_copy(d, False).wait_recv()

    def forward_group(g, total):
        base = g * GROUP
        sides = [col_side[col_s[0, base + j]] for j in range(GROUP)]
        terms = [
            lax.dot_general(sides[j], blk[base + j], (((1,), (1,)), ((), ())), preferred_element_type=f32)
            for j in range(GROUP)
        ]
        for j in range(GROUP):
            total = total * table_s[0, base + j].astype(f32) + terms[j]
            run[base + j] = total
        return total

    total = jnp.zeros(run.shape[1:], f32)
    for k in range(chunks):
        chunk_copy(k).wait()
        total = lax.fori_loop(k * per // GROUP, (k + 1) * per // GROUP, forward_group, total)

    @pl.loop(0, n_col)
    def _(p):
        for u in range(seg):
            first, last = ptr_s[0, p * seg + u], ptr_s[0, p * seg + u + 1]
            fwd[p % 2, p // 2, u] = run[jnp.where(last > first, last - 1, slots)]

    near_copy = pltpu.make_async_remote_copy(
        src_ref=fwd.at[1 - core], dst_ref=near, send_sem=near_send, recv_sem=near_recv,
        device_id=(r, z * 2 + 1 - core), device_id_type=MESH)
    near_copy.start()

    @pl.loop(1, n_col)
    def _(d):
        rs_copy(d, False).wait_recv()

    def backward_group(g, total):
        base = g * GROUP
        sides = [row_side[table_s[2, base + j]] for j in range(GROUP)]
        terms = [
            lax.dot_general(
                sides[j], blk[table_s[1, base + j]], (((1,), (0,)), ((), ())), preferred_element_type=f32)
            for j in range(GROUP)
        ]
        for j in range(GROUP):
            total = total * table_s[3, base + j].astype(f32) + terms[j]
            run[base + j] = total
        return total

    def f_copy(d, mine):
        to = (z + d) % nz
        return pltpu.make_async_remote_copy(
            src_ref=fwd.at[core, to], dst_ref=fwd_in.at[z if mine else (z + nz - d) % nz],
            send_sem=f_send.at[d], recv_sem=f_recv.at[d],
            device_id=(r, to * 2 + core), device_id_type=MESH)

    groups = slots // GROUP
    early = max(groups // 3, 1)
    total = lax.fori_loop(0, early, backward_group, jnp.zeros(run.shape[1:], f32))
    near_copy.wait()

    @pl.loop(0, nz)
    def _(p):
        fwd[core, p] = fwd[core, p] + near[p]

    @pl.loop(1, nz)
    def _(d):
        f_copy(d, True).start()

    lax.fori_loop(early, groups, backward_group, total)

    @pl.loop(0, n_row)
    def _(p):
        for u in range(seg):
            q = p * seg + u
            last = table_s[4, q]
            first = jnp.where(q > 0, table_s[4, jnp.maximum(q - 1, 0)], 0)
            bwd[p, u] = run[jnp.where(last > first, last - 1, slots)]

    def b_copy(d, mine):
        to = (r + d) % n_row
        return pltpu.make_async_remote_copy(
            src_ref=bwd.at[to], dst_ref=bwd_in.at[r if mine else (r + n_row - d) % n_row],
            send_sem=b_send.at[d], recv_sem=b_recv.at[d],
            device_id=(to, c), device_id_type=MESH)

    @pl.loop(1, n_row)
    def _(d):
        b_copy(d, True).start()

    bwd_in[r] = bwd[r]
    fwd_in[z] = fwd[core, z]

    @pl.loop(1, nz)
    def _(d):
        f_copy(d, False).wait_recv()

    parts = [fwd_in[p] for p in range(nz)]

    @pl.loop(1, n_row)
    def _(d):
        b_copy(d, False).wait_recv()

    parts = parts + [bwd_in[p] for p in range(n_row)]
    result = functools.reduce(lambda a, b: a + b, parts)
    for u in range(seg):
        out_ref[:, u * 128:(u + 1) * 128] = result[u]

    @pl.loop(1, n_row)
    def _(d):
        cs_copy(d, True).wait_send()
        b_copy(d, True).wait_send()

    @pl.loop(1, n_col)
    def _(d):
        rs_copy(d, True).wait_send()

    @pl.loop(1, nz)
    def _(d):
        f_copy(d, True).wait_send()


def body(n_row, n_col, vectors, blocks, row_ptr, col_idx):
    count, segment = vectors.shape
    slots, edge = blocks.shape[1], blocks.shape[2]
    seg = segment // edge
    chunks = 6 if slots % (6 * GROUP) == 0 else 1
    i32, f32, bf16 = jnp.int32, jnp.float32, jnp.bfloat16
    width = -(-max(slots, n_row * seg) // 128) * 128
    nz = n_col // 2
    dma = pltpu.SemaphoreType.DMA
    anywhere = pl.BlockSpec(memory_space=pl.ANY)
    return pl.pallas_call(
        functools.partial(kernel, n_row, n_col, chunks),
        out_shape=jax.ShapeDtypeStruct((count, segment), f32),
        in_specs=[anywhere] * 4,
        out_specs=pl.BlockSpec(memory_space=pltpu.VMEM),
        scratch_shapes=[
            pltpu.VMEM((count, segment), bf16),
            pltpu.VMEM((slots, edge, edge), bf16),
            pltpu.SMEM(row_ptr.shape, i32),
            pltpu.SMEM(col_idx.shape, i32),
            pltpu.VMEM(row_ptr.shape, i32),
            pltpu.VMEM(col_idx.shape, i32),
            pltpu.VMEM((8, width), i32),
            pltpu.SMEM((8, width), i32),
            pltpu.VMEM((n_col * seg, count, edge), bf16),
            pltpu.VMEM((n_row * seg, count, edge), bf16),
            pltpu.VMEM((slots + 1, count, edge), f32),
            pltpu.VMEM((2, nz, seg, count, edge), f32),
            pltpu.VMEM((n_row, seg, count, edge), f32),
            pltpu.VMEM((nz, seg, count, edge), f32),
            pltpu.VMEM((nz, seg, count, edge), f32),
            pltpu.VMEM((n_row, seg, count, edge), f32),
            dma, dma((chunks,)), dma((4,)),
            dma((n_col,)), dma((n_col,)), dma((n_row,)), dma((n_row,)), dma, dma,
            dma((nz,)), dma((nz,)), dma((n_row,)), dma((n_row,)),
        ],
        compiler_params=pltpu.CompilerParams(
            collective_id=0, has_side_effects=True, vmem_limit_bytes=40 * 1024 * 1024),
        cost_estimate=pl.CostEstimate(
            flops=4 * slots * count * edge * edge, bytes_accessed=2 * slots * edge * edge, transcendentals=0),
    )(vectors, blocks, row_ptr, col_idx)


def solution(mesh):
    in_specs = (
        P(None, ("row", "col")),
        P("row", "col", None, None),
        P("row", "col"),
        P("row", "col"),
    )
    out_specs = P(None, ("row", "col"))
    shape = dict(mesh.shape)
    return jax.shard_map(
        functools.partial(body, shape["row"], shape["col"]),
        mesh=mesh, in_specs=in_specs, out_specs=out_specs, check_vma=False)
```

time: 130 us -> 27.4 us (0.21)
  blocking collectives: 45.5 us -> 0 us
  waiting for transfers between devices: 37 us -> 0 us
  Pallas kernels: 0 us -> 21.7 us
  other arithmetic: 17.8 us -> 0 us
  between operations: 13.6 us -> 0.01 us
  matrix products: 10.1 us -> 0 us
    all_gather x1 -> x0, blocking collectives: 45.5 us -> none  [body(): everything = lax.all_gather(vectors, ('row', 'col'), axis=1, tiled=True)]
    reduce_scatter x2 -> x0, waiting for transfers between devices: 37 us -> none  [the longest x1 32.8 us: body(): lax.psum_scatter(forward_sum, 'col', scatter_dimension=0, tiled=True)]
    pallas_call x0 -> x1, Pallas kernels: none -> 21.7 us  [body(): pl.pallas_call(functools.partial(kernel, n_row, n_col, chunks), out_shape...]
    scatter-add x2 -> x0, other arithmetic: 15.6 us -> none  [the longest x1 7.97 us: tile_terms(): jax.ops.segment_sum(forward, slot_rows, num_segments=row_blocks.shape[1],...]
    dot_general x2 -> x0, matrix products: 10.1 us -> none  [the longest x1 5.84 us: tile_terms(): jnp.einsum('ksj,sij->ski', picked_cols, tile_blocks, preferred_element_ty...]
    unnamed x7 -> x9, local copies, waits for them, and re-layouts: 1.5 us -> 5.45 us
    gather x2 -> x0, local copies, waits for them, and re-layouts: 1.57 us -> none  [the longest x1 0.79 us: tile_terms(): picked_cols = jnp.take(col_blocks, columns, axis=1)]
    reshape x1 -> x0, other arithmetic: 1.39 us -> none  [body(): return combined.transpose(1, 0, 2).reshape(count_vectors, segment)]
  transfers between devices with their start and end apart: 2 -> 0, of which waited for: 2 -> 0; matrix products, arithmetic and copies ran while one was open for 12% -> 0% of each run, Pallas kernels for 0% -> 0%
where the time goes in v1:
time: 27.4 us; the launch traced here: 27.2 us
  Pallas kernels  21.7 us (79%)
  local copies, waits for them, and re-layouts  5.45 us (20%)
    pallas_call x1, Pallas kernels, body(): pl.pallas_call(functools.partial(kernel, n_row, n_col, chunks), out_shape...  21.7 us
    unnamed x9, local copies, waits for them, and re-layouts  5.45 us

profile of v1, /device:TPU:0, one launch (start us, length us, event | category | flops | bytes accessed | tf_op | source)
XLA Modules:
  0.0 27.2 jit_solution(1858829722327030986)
XLA Ops:
  0.0 0.0 copy-start
  0.0 2.8 %copy-done = bf16[1,192,128,128]{3,2,1,0:T(8,128)(2,1)S(1)} copy-done((bf16[1,192,128,128]{3,2,1,0:T(8,128)(2,1)S(1)}, bf16[1,192,128,128]{3,2,1,0:T(8,128)(2,1)}, u32[]{:S(2)}) %copy-start) | copy-done | bytes 6291480
  2.8 0.0 copy-start.1
  2.8 0.7 %copy-done.1 = bf16[16,512]{1,0:T(8,128)(2,1)S(1)} copy-done((bf16[16,512]{1,0:T(8,128)(2,1)S(1)}, bf16[16,512]{1,0:T(8,128)(2,1)}, u32[]{:S(2)}) %copy-start.1) | copy-done | bytes 16408
  3.5 0.0 copy-start.2
  3.5 0.7 %copy-done.2 = s32[1,192]{1,0:T(1,128)S(1)} copy-done((s32[1,192]{1,0:T(1,128)S(1)}, s32[1,192]{1,0:T(1,128)}, u32[]{:S(2)}) %copy-start.2) | copy-done | bytes 792
  4.2 0.0 copy-start.3
  4.2 0.7 %copy-done.3 = s32[1,33]{1,0:T(1,128)S(1)} copy-done((s32[1,33]{1,0:T(1,128)S(1)}, s32[1,33]{1,0:T(1,128)}, u32[]{:S(2)}) %copy-start.3) | copy-done | bytes 156
  4.8 21.7 %shard_map.46 = f32[16,512]{1,0:T(8,128)S(1)} custom-call(bf16[16,512]{1,0:T(8,128)(2,1)S(1)} %copy-done.1, bf16[1,192,128,128]{3,2,1,0:T(8,128)(2,1)S(1)} %copy-done, s32[1,33]{1,0:T(1,128)S(1)} %copy-done.3, s32[1,192]{1,0:T(1,128)S(1)} %copy-done.2), custom_call_target="tpu_custom_call" | custom-call | flops 201326592 | bytes 6291456 | tf_op jit(solution)/shard_map/pallas_call | solution.py:276
  26.6 0.6 %copy.6 = f32[16,512]{1,0:T(8,128)} copy(f32[16,512]{1,0:T(8,128)S(1)} %shard_map.46) | data formatting | bytes 65536
Async XLA Ops:
  0.0 2.8 %copy-start = (bf16[1,192,128,128]{3,2,1,0:T(8,128)(2,1)S(1)}, bf16[1,192,128,128]{3,2,1,0:T(8,128)(2,1)}, u32[]{:S(2)}) copy-start(bf16[1,192,128,128]{3,2,1,0:T(8,128)(2,1)} %blk_hbm.1) | copy-start | bytes 18874372
  2.8 0.7 %copy-start.1 = (bf16[16,512]{1,0:T(8,128)(2,1)S(1)}, bf16[16,512]{1,0:T(8,128)(2,1)}, u32[]{:S(2)}) copy-start(bf16[16,512]{1,0:T(8,128)(2,1)} %vec_hbm.1) | copy-start | bytes 49156
  3.5 0.7 %copy-start.2 = (s32[1,192]{1,0:T(1,128)S(1)}, s32[1,192]{1,0:T(1,128)}, u32[]{:S(2)}) copy-start(s32[1,192]{1,0:T(1,128)} %col_hbm.1) | copy-start | bytes 2308
  4.2 0.7 %copy-start.3 = (s32[1,33]{1,0:T(1,128)S(1)}, s32[1,33]{1,0:T(1,128)}, u32[]{:S(2)}) copy-start(s32[1,33]{1,0:T(1,128)} %ptr_hbm.1) | copy-start | bytes 400

commit v2 on v1

--- a/solution.py
+++ b/solution.py
@@ -1,4 +1,5 @@
 import functools
+import math
 
 import jax
 import jax.numpy as jnp
@@ -8,7 +9,7 @@
 from jax.sharding import PartitionSpec as P
 
 MESH = pl.DeviceIdType.MESH
-GROUP = 16
+GROUP = 48
 FAR = 1 << 20
 
 
@@ -54,7 +55,7 @@
 
 
 def kernel(
-    n_row, n_col, chunks,
+    n_row, n_col, chunks, group,
     vec_hbm, blk_hbm, ptr_hbm, col_hbm, out_ref,
     vec, blk, ptr_s, col_s, ptr_v, col_v, table_v, table_s,
     row_side, col_side, run, fwd, bwd, near, fwd_in, bwd_in,
@@ -73,6 +74,16 @@
 
     get_vec = pltpu.make_async_copy(vec_hbm, vec, vec_sem)
     get_vec.start()
+    barrier = pltpu.get_barrier_semaphore()
+
+    @pl.loop(1, n_row)
+    def _(d):
+        pl.semaphore_signal(barrier, inc=1, device_id=((r + d) % n_row, c), device_id_type=MESH)
+
+    @pl.loop(1, n_col)
+    def _(d):
+        pl.semaphore_signal(barrier, inc=1, device_id=(r, (c + d) % n_col), device_id_type=MESH)
+
     index_copies = [
         pltpu.make_async_copy(src, dst, idx_sem.at[k])
         for k, (src, dst) in enumerate(
@@ -88,16 +99,6 @@
 
     for k in range(chunks):
         chunk_copy(k).start()
-
-    barrier = pltpu.get_barrier_semaphore()
-
-    @pl.loop(1, n_row)
-    def _(d):
-        pl.semaphore_signal(barrier, inc=1, device_id=((r + d) % n_row, c), device_id_type=MESH)
-
-    @pl.loop(1, n_col)
-    def _(d):
-        pl.semaphore_signal(barrier, inc=1, device_id=(r, (c + d) % n_col), device_id_type=MESH)
 
     get_vec.wait()
     for u in range(seg):
@@ -145,22 +146,42 @@
     def _(d):
         cs_copy(d, False).wait_recv()
 
-    def forward_group(g, total):
-        base = g * GROUP
-        sides = [col_side[col_s[0, base + j]] for j in range(GROUP)]
-        terms = [
-            lax.dot_general(sides[j], blk[base + j], (((1,), (1,)), ((), ())), preferred_element_type=f32)
-            for j in range(GROUP)
-        ]
-        for j in range(GROUP):
-            total = total * table_s[0, base + j].astype(f32) + terms[j]
-            run[base + j] = total
-        return total
+    def four_terms(sides, tiles, across):
+        if len(sides) != 4:
+            return [
+                lax.dot_general(x, t, (((1,), (across,)), ((), ())), preferred_element_type=f32)
+                for x, t in zip(sides, tiles)
+            ]
+        none = jnp.zeros_like(sides[0])
+        rows = [[sides[0], none], [sides[1], none], [none, sides[2]], [none, sides[3]]]
+        left = jnp.concatenate([jnp.concatenate(pair, 1) for pair in rows], 0)
+        places = ((0, 2), (1, 3)) if across else ((0, 1), (2, 3))
+        right = jnp.concatenate([jnp.concatenate([tiles[k] for k in pair], 1) for pair in places], 0)
+        out = lax.dot_general(left, right, (((1,), (across,)), ((), ())), preferred_element_type=f32)
+        m, n = none.shape
+        return [out[k * m:(k + 1) * m, (k % 2) * n:(k % 2 + 1) * n] for k in range(4)]
+
+    step = math.gcd(group, 4)
+
+    def group_loop(side_of, tile_of, keep_row, across):
+        def one_group(g, total):
+            for j in range(0, group, step):
+                ids = [g * group + j + k for k in range(step)]
+                terms = four_terms([side_of(s) for s in ids], [tile_of(s) for s in ids], across)
+                for s, term in zip(ids, terms):
+                    total = total * table_s[keep_row, s].astype(f32) + term
+                    run[s] = total
+            return total
+        return one_group
+
+    forward_group = group_loop(lambda s: col_side[col_s[0, s]], lambda s: blk[s], 0, 1)
+    backward_group = group_loop(
+        lambda s: row_side[table_s[2, s]], lambda s: blk[table_s[1, s]], 3, 0)
 
     total = jnp.zeros(run.shape[1:], f32)
     for k in range(chunks):
         chunk_copy(k).wait()
-        total = lax.fori_loop(k * per // GROUP, (k + 1) * per // GROUP, forward_group, total)
+        total = lax.fori_loop(k * per // group, (k + 1) * per // group, forward_group, total)
 
     @pl.loop(0, n_col)
     def _(p):
@@ -176,19 +197,6 @@
     @pl.loop(1, n_col)
     def _(d):
         rs_copy(d, False).wait_recv()
-
-    def backward_group(g, total):
-        base = g * GROUP
-        sides = [row_side[table_s[2, base + j]] for j in range(GROUP)]
-        terms = [
-            lax.dot_general(
-                sides[j], blk[table_s[1, base + j]], (((1,), (0,)), ((), ())), preferred_element_type=f32)
-            for j in range(GROUP)
-        ]
-        for j in range(GROUP):
-            total = total * table_s[3, base + j].astype(f32) + terms[j]
-            run[base + j] = total
-        return total
 
     def f_copy(d, mine):
         to = (z + d) % nz
@@ -197,8 +205,8 @@
             send_sem=f_send.at[d], recv_sem=f_recv.at[d],
             device_id=(r, to * 2 + core), device_id_type=MESH)
 
-    groups = slots // GROUP
-    early = max(groups // 3, 1)
+    groups = slots // group
+    early = max(groups // 4, 1)
     total = lax.fori_loop(0, early, backward_group, jnp.zeros(run.shape[1:], f32))
     near_copy.wait()
 
@@ -267,14 +275,15 @@
     count, segment = vectors.shape
     slots, edge = blocks.shape[1], blocks.shape[2]
     seg = segment // edge
-    chunks = 6 if slots % (6 * GROUP) == 0 else 1
+    group = math.gcd(slots, GROUP)
+    chunks = slots // group
     i32, f32, bf16 = jnp.int32, jnp.float32, jnp.bfloat16
     width = -(-max(slots, n_row * seg) // 128) * 128
     nz = n_col // 2
     dma = pltpu.SemaphoreType.DMA
-    anywhere = pl.BlockSpec(memory_space=pl.ANY)
+    anywhere = pl.BlockSpec(memory_space=pltpu.HBM)
     return pl.pallas_call(
-        functools.partial(kernel, n_row, n_col, chunks),
+        functools.partial(kernel, n_row, n_col, chunks, group),
         out_shape=jax.ShapeDtypeStruct((count, segment), f32),
         in_specs=[anywhere] * 4,
         out_specs=pl.BlockSpec(memory_space=pltpu.VMEM),
@@ -300,7 +309,7 @@
             dma((nz,)), dma((nz,)), dma((n_row,)), dma((n_row,)),
         ],
         compiler_params=pltpu.CompilerParams(
-            collective_id=0, has_side_effects=True, vmem_limit_bytes=40 * 1024 * 1024),
+            collective_id=0, has_side_effects=True, vmem_limit_bytes=60 * 1024 * 1024),
         cost_estimate=pl.CostEstimate(
             flops=4 * slots * count * edge * edge, bytes_accessed=2 * slots * edge * edge, transcendentals=0),
     )(vectors, blocks, row_ptr, col_idx)

time: 27.4 us -> 20.4 us (0.74)
  local copies, waits for them, and re-layouts: 5.45 us -> 1.38 us
  Pallas kernels: 21.7 us -> 18.7 us
    unnamed x9 -> x1, local copies, waits for them, and re-layouts: 5.45 us -> 1.38 us
    pallas_call x1, Pallas kernels: 21.7 us -> 18.7 us  [body(): pl.pallas_call(functools.partial(kernel, n_row, n_col, chunks, group), ou...]
where the time goes in v2:
time: 20.4 us; the launch traced here: 20.1 us
  Pallas kernels  18.7 us (92%)
  local copies, waits for them, and re-layouts  1.38 us (7%)
    pallas_call x1, Pallas kernels, body(): pl.pallas_call(functools.partial(kernel, n_row, n_col, chunks, group), ou...  18.7 us
    unnamed x1, local copies, waits for them, and re-layouts  1.38 us

profile of v2, /device:TPU:0, one launch (start us, length us, event | category | flops | bytes accessed | tf_op | source)
XLA Modules:
  0.0 20.1 jit_solution(2491616030311592430)
XLA Ops:
  0.0 18.7 %shard_map.46 = f32[16,512]{1,0:T(8,128)} custom-call(bf16[16,512]{1,0:T(8,128)(2,1)} %vec_hbm.1, bf16[1,192,128,128]{3,2,1,0:T(8,128)(2,1)} %blk_hbm.1, s32[1,33]{1,0:T(1,128)} %ptr_hbm.1, s32[1,192]{1,0:T(1,128)} %col_hbm.1), custom_call_target="tpu_custom_call" | custom-call | flops 201326592 | bytes 6291456 | tf_op jit(solution)/shard_map/pallas_call | solution.py:285
  18.8 1.4 %copy.6 = f32[16,512]{1,0:T(8,128)} copy(f32[16,512]{1,0:T(8,128)} %shard_map.46) | data formatting | bytes 65536

commit v3 on v2

--- a/solution.py
+++ b/solution.py
@@ -27,8 +27,8 @@
     def count(mask, axis):
         return total(jnp.where(mask, 1, 0), axis)
 
-    edge = (tile_rows + 1, tile_rows + 1)
-    pointer_col = total(jnp.where(iota(edge, 0) == iota(edge, 1), pointers, 0), 1)
+    corner = (tile_rows + 1, tile_rows + 1)
+    pointer_col = total(jnp.where(iota(corner, 0) == iota(corner, 1), pointers, 0), 1)
     wide = (tile_rows + 1, slots)
     rows = count(pointer_col <= iota(wide, 1), 0) - 1
     keep_row = jnp.where(count(pointer_col == iota(wide, 1), 0) == 0, 1, 0)
@@ -57,9 +57,9 @@
 def kernel(
     n_row, n_col, chunks, group,
     vec_hbm, blk_hbm, ptr_hbm, col_hbm, out_ref,
-    vec, blk, ptr_s, col_s, ptr_v, col_v, table_v, table_s,
-    row_side, col_side, run, fwd, bwd, near, fwd_in, bwd_in,
-    vec_sem, blk_sem, idx_sem,
+    blk, ptr_s, col_s, ptr_v, col_v, table_v, table_s,
+    row_side, col_side, row_blocks, col_blocks, run, fwd, bwd, near, fwd_in, bwd_in,
+    here, vec_sem, blk_sem, idx_sem,
     rs_send, rs_recv, cs_send, cs_recv, near_send, near_recv,
     f_send, f_recv, b_send, b_recv,
 ):
@@ -67,30 +67,33 @@
     c = lax.axis_index("col")
     z, core = c // 2, c % 2
     nz = n_col // 2
-    seg = vec.shape[1] // 128
+    edge = blk.shape[1]
+    seg = vec_hbm.shape[1] // edge
     slots = blk.shape[0]
     per = slots // chunks
     f32 = jnp.float32
 
-    get_vec = pltpu.make_async_copy(vec_hbm, vec, vec_sem)
-    get_vec.start()
     barrier = pltpu.get_barrier_semaphore()
 
     @pl.loop(1, n_row)
     def _(d):
         pl.semaphore_signal(barrier, inc=1, device_id=((r + d) % n_row, c), device_id_type=MESH)
 
-    @pl.loop(1, n_col)
-    def _(d):
-        pl.semaphore_signal(barrier, inc=1, device_id=(r, (c + d) % n_col), device_id_type=MESH)
-
+    @pl.loop(c + 1, n_col)
+    def _(p):
+        pl.semaphore_signal(barrier, inc=1, device_id=(r, p), device_id_type=MESH)
+
+    own_copies = [
+        pltpu.make_async_copy(vec_hbm, dst, vec_sem.at[k])
+        for k, dst in enumerate((col_side.at[r], row_side.at[c]))
+    ]
     index_copies = [
         pltpu.make_async_copy(src, dst, idx_sem.at[k])
         for k, (src, dst) in enumerate(
             ((ptr_hbm, ptr_v), (col_hbm, col_v), (ptr_hbm, ptr_s), (col_hbm, col_s))
         )
     ]
-    for copy in index_copies:
+    for copy in index_copies + own_copies:
         copy.start()
 
     def chunk_copy(k):
@@ -100,36 +103,29 @@
     for k in range(chunks):
         chunk_copy(k).start()
 
-    get_vec.wait()
-    for u in range(seg):
-        piece = vec[:, u * 128:(u + 1) * 128]
-        row_side[c * seg + u] = piece
-        col_side[r * seg + u] = piece
-    pl.semaphore_wait(barrier, n_row + n_col - 2)
+    pl.semaphore_wait(barrier, n_row - 1 + c)
 
     def cs_copy(d, mine):
         owner = r if mine else (r + n_row - d) % n_row
-        part = pl.ds(owner * seg, seg)
         return pltpu.make_async_remote_copy(
-            src_ref=col_side.at[part], dst_ref=col_side.at[part],
+            src_ref=vec_hbm, dst_ref=col_side.at[owner],
             send_sem=cs_send.at[d], recv_sem=cs_recv.at[d],
             device_id=((r + d) % n_row, c), device_id_type=MESH)
 
-    def rs_copy(d, mine):
-        owner = c if mine else (c + n_col - d) % n_col
-        part = pl.ds(owner * seg, seg)
+    def rs_copy(to, source):
         return pltpu.make_async_remote_copy(
-            src_ref=row_side.at[part], dst_ref=row_side.at[part],
-            send_sem=rs_send.at[d], recv_sem=rs_recv.at[d],
-            device_id=(r, (c + d) % n_col), device_id_type=MESH)
+            src_ref=vec_hbm, dst_ref=row_side.at[source],
+            send_sem=rs_send.at[to], recv_sem=rs_recv.at[source],
+            device_id=(r, to), device_id_type=MESH)
 
     @pl.loop(1, n_row)
     def _(d):
         cs_copy(d, True).start()
 
-    @pl.loop(1, n_col)
-    def _(d):
-        rs_copy(d, True).start()
+    @pl.loop(0, c)
+    def _(p):
+        pl.semaphore_signal(here, inc=1, device_id=(r, p), device_id_type=MESH)
+        rs_copy(p, c).start()
 
     for copy in index_copies:
         copy.wait()
@@ -145,6 +141,9 @@
     @pl.loop(1, n_row)
     def _(d):
         cs_copy(d, False).wait_recv()
+
+    for copy in own_copies:
+        copy.wait()
 
     def four_terms(sides, tiles, across):
         if len(sides) != 4:
@@ -174,10 +173,17 @@
             return total
         return one_group
 
-    forward_group = group_loop(lambda s: col_side[col_s[0, s]], lambda s: blk[s], 0, 1)
+    def split(side, out, owners):
+        @pl.loop(0, owners)
+        def _(p):
+            for u in range(seg):
+                out[p * seg + u] = side[p, :, u * edge:(u + 1) * edge]
+
+    forward_group = group_loop(lambda s: col_blocks[col_s[0, s]], lambda s: blk[s], 0, 1)
     backward_group = group_loop(
-        lambda s: row_side[table_s[2, s]], lambda s: blk[table_s[1, s]], 3, 0)
-
+        lambda s: row_blocks[table_s[2, s]], lambda s: blk[table_s[1, s]], 3, 0)
+
+    split(col_side, col_blocks, n_row)
     total = jnp.zeros(run.shape[1:], f32)
     for k in range(chunks):
         chunk_copy(k).wait()
@@ -189,6 +195,14 @@
             first, last = ptr_s[0, p * seg + u], ptr_s[0, p * seg + u + 1]
             fwd[p % 2, p // 2, u] = run[jnp.where(last > first, last - 1, slots)]
 
+    @pl.when(c < n_col - 1)
+    def _():
+        pl.semaphore_wait(here, n_col - 1 - c)
+
+    @pl.loop(c + 1, n_col)
+    def _(p):
+        rs_copy(p, c).start()
+
     near_copy = pltpu.make_async_remote_copy(
         src_ref=fwd.at[1 - core], dst_ref=near, send_sem=near_send, recv_sem=near_recv,
         device_id=(r, z * 2 + 1 - core), device_id_type=MESH)
@@ -196,7 +210,10 @@
 
     @pl.loop(1, n_col)
     def _(d):
-        rs_copy(d, False).wait_recv()
+        p = (c + d) % n_col
+        rs_copy(p, p).wait_recv()
+
+    split(row_side, row_blocks, n_col)
 
     def f_copy(d, mine):
         to = (z + d) % nz
@@ -264,7 +281,7 @@
 
     @pl.loop(1, n_col)
     def _(d):
-        rs_copy(d, True).wait_send()
+        rs_copy((c + d) % n_col, c).wait_send()
 
     @pl.loop(1, nz)
     def _(d):
@@ -288,7 +305,6 @@
         in_specs=[anywhere] * 4,
         out_specs=pl.BlockSpec(memory_space=pltpu.VMEM),
         scratch_shapes=[
-            pltpu.VMEM((count, segment), bf16),
             pltpu.VMEM((slots, edge, edge), bf16),
             pltpu.SMEM(row_ptr.shape, i32),
             pltpu.SMEM(col_idx.shape, i32),
@@ -296,6 +312,8 @@
             pltpu.VMEM(col_idx.shape, i32),
             pltpu.VMEM((8, width), i32),
             pltpu.SMEM((8, width), i32),
+            pltpu.VMEM((n_col, count, segment), bf16),
+            pltpu.VMEM((n_row, count, segment), bf16),
             pltpu.VMEM((n_col * seg, count, edge), bf16),
             pltpu.VMEM((n_row * seg, count, edge), bf16),
             pltpu.VMEM((slots + 1, count, edge), f32),
@@ -304,7 +322,7 @@
             pltpu.VMEM((nz, seg, count, edge), f32),
             pltpu.VMEM((nz, seg, count, edge), f32),
             pltpu.VMEM((n_row, seg, count, edge), f32),
-            dma, dma((chunks,)), dma((4,)),
+            pltpu.SemaphoreType.REGULAR, dma((2,)), dma((chunks,)), dma((4,)),
             dma((n_col,)), dma((n_col,)), dma((n_row,)), dma((n_row,)), dma, dma,
             dma((nz,)), dma((nz,)), dma((n_row,)), dma((n_row,)),
         ],

time: 20.4 us -> 21.6 us (1.059)
  Pallas kernels: 18.7 us -> 20 us
    pallas_call x1, Pallas kernels: 18.7 us -> 20 us  [body(): pl.pallas_call(functools.partial(kernel, n_row, n_col, chunks, group), ou...]
where the time goes in v3:
time: 21.6 us; the launch traced here: 21.4 us
  Pallas kernels  20 us (93%)
  local copies, waits for them, and re-layouts  1.38 us (6%)
    pallas_call x1, Pallas kernels, body(): pl.pallas_call(functools.partial(kernel, n_row, n_col, chunks, group), ou...  20 us
    unnamed x1, local copies, waits for them, and re-layouts  1.38 us

profile of v3, /device:TPU:0, one launch (start us, length us, event | category | flops | bytes accessed | tf_op | source)
XLA Modules:
  0.0 21.4 jit_solution(12277963256474074911)
XLA Ops:
  0.0 20.0 %shard_map.46 = f32[16,512]{1,0:T(8,128)} custom-call(bf16[16,512]{1,0:T(8,128)(2,1)} %vec_hbm.1, bf16[1,192,128,128]{3,2,1,0:T(8,128)(2,1)} %blk_hbm.1, s32[1,33]{1,0:T(1,128)} %ptr_hbm.1, s32[1,192]{1,0:T(1,128)} %col_hbm.1), custom_call_target="tpu_custom_call" | custom-call | flops 201326592 | bytes 6291456 | tf_op jit(solution)/shard_map/pallas_call | solution.py:302
  20.0 1.4 %copy.6 = f32[16,512]{1,0:T(8,128)} copy(f32[16,512]{1,0:T(8,128)} %shard_map.46) | data formatting | bytes 65536

commit v4 on v3

--- a/solution.py
+++ b/solution.py
@@ -73,48 +73,50 @@
     per = slots // chunks
     f32 = jnp.float32
 
-    barrier = pltpu.get_barrier_semaphore()
-
-    @pl.loop(1, n_row)
-    def _(d):
-        pl.semaphore_signal(barrier, inc=1, device_id=((r + d) % n_row, c), device_id_type=MESH)
-
-    @pl.loop(c + 1, n_col)
-    def _(p):
-        pl.semaphore_signal(barrier, inc=1, device_id=(r, p), device_id_type=MESH)
-
     own_copies = [
         pltpu.make_async_copy(vec_hbm, dst, vec_sem.at[k])
         for k, dst in enumerate((col_side.at[r], row_side.at[c]))
     ]
+    for copy in own_copies:
+        copy.start()
+
+    barrier = pltpu.get_barrier_semaphore()
+
+    @pl.loop(1, n_row)
+    def _(d):
+        pl.semaphore_signal(barrier, inc=1, device_id=((r + d) % n_row, c), device_id_type=MESH)
+
+    @pl.loop(c + 1, n_col)
+    def _(p):
+        pl.semaphore_signal(barrier, inc=1, device_id=(r, p), device_id_type=MESH)
+
     index_copies = [
         pltpu.make_async_copy(src, dst, idx_sem.at[k])
         for k, (src, dst) in enumerate(
             ((ptr_hbm, ptr_v), (col_hbm, col_v), (ptr_hbm, ptr_s), (col_hbm, col_s))
         )
     ]
-    for copy in index_copies + own_copies:
+    for copy in index_copies:
         copy.start()
 
     def chunk_copy(k):
         part = pl.ds(k * per, per)
         return pltpu.make_async_copy(blk_hbm.at[0, part], blk.at[part], blk_sem.at[k])
 
-    for k in range(chunks):
-        chunk_copy(k).start()
-
+    for copy in own_copies:
+        copy.wait()
     pl.semaphore_wait(barrier, n_row - 1 + c)
 
     def cs_copy(d, mine):
         owner = r if mine else (r + n_row - d) % n_row
         return pltpu.make_async_remote_copy(
-            src_ref=vec_hbm, dst_ref=col_side.at[owner],
+            src_ref=col_side.at[r], dst_ref=col_side.at[owner],
             send_sem=cs_send.at[d], recv_sem=cs_recv.at[d],
             device_id=((r + d) % n_row, c), device_id_type=MESH)
 
     def rs_copy(to, source):
         return pltpu.make_async_remote_copy(
-            src_ref=vec_hbm, dst_ref=row_side.at[source],
+            src_ref=row_side.at[c], dst_ref=row_side.at[source],
             send_sem=rs_send.at[to], recv_sem=rs_recv.at[source],
             device_id=(r, to), device_id_type=MESH)
 
@@ -126,6 +128,9 @@
     def _(p):
         pl.semaphore_signal(here, inc=1, device_id=(r, p), device_id_type=MESH)
         rs_copy(p, c).start()
+
+    for k in range(chunks):
+        chunk_copy(k).start()
 
     for copy in index_copies:
         copy.wait()
@@ -141,9 +146,6 @@
     @pl.loop(1, n_row)
     def _(d):
         cs_copy(d, False).wait_recv()
-
-    for copy in own_copies:
-        copy.wait()
 
     def four_terms(sides, tiles, across):
         if len(sides) != 4:
@@ -188,20 +190,20 @@
     for k in range(chunks):
         chunk_copy(k).wait()
         total = lax.fori_loop(k * per // group, (k + 1) * per // group, forward_group, total)
+        if k == (chunks - 1) // 2:
+            @pl.when(c < n_col - 1)
+            def _():
+                pl.semaphore_wait(here, n_col - 1 - c)
+
+            @pl.loop(c + 1, n_col)
+            def _(p):
+                rs_copy(p, c).start()
 
     @pl.loop(0, n_col)
     def _(p):
         for u in range(seg):
             first, last = ptr_s[0, p * seg + u], ptr_s[0, p * seg + u + 1]
             fwd[p % 2, p // 2, u] = run[jnp.where(last > first, last - 1, slots)]
-
-    @pl.when(c < n_col - 1)
-    def _():
-        pl.semaphore_wait(here, n_col - 1 - c)
-
-    @pl.loop(c + 1, n_col)
-    def _(p):
-        rs_copy(p, c).start()
 
     near_copy = pltpu.make_async_remote_copy(
         src_ref=fwd.at[1 - core], dst_ref=near, send_sem=near_send, recv_sem=near_recv,

time: 21.6 us -> 20.2 us (0.935)
  Pallas kernels: 20 us -> 18.6 us
    pallas_call x1, Pallas kernels: 20 us -> 18.6 us  [body(): pl.pallas_call(functools.partial(kernel, n_row, n_col, chunks, group), ou...]
where the time goes in v4:
time: 20.2 us; the launch traced here: 20 us
  Pallas kernels  18.6 us (92%)
  local copies, waits for them, and re-layouts  1.38 us (7%)
    pallas_call x1, Pallas kernels, body(): pl.pallas_call(functools.partial(kernel, n_row, n_col, chunks, group), ou...  18.6 us
    unnamed x1, local copies, waits for them, and re-layouts  1.38 us

profile of v4, /device:TPU:0, one launch (start us, length us, event | category | flops | bytes accessed | tf_op | source)
XLA Modules:
  0.0 20.0 jit_solution(13694855504896018724)
XLA Ops:
  0.0 18.6 %shard_map.46 = f32[16,512]{1,0:T(8,128)} custom-call(bf16[16,512]{1,0:T(8,128)(2,1)} %vec_hbm.1, bf16[1,192,128,128]{3,2,1,0:T(8,128)(2,1)} %blk_hbm.1, s32[1,33]{1,0:T(1,128)} %ptr_hbm.1, s32[1,192]{1,0:T(1,128)} %col_hbm.1), custom_call_target="tpu_custom_call" | custom-call | flops 201326592 | bytes 6291456 | tf_op jit(solution)/shard_map/pallas_call | solution.py:304
  18.6 1.4 %copy.6 = f32[16,512]{1,0:T(8,128)} copy(f32[16,512]{1,0:T(8,128)} %shard_map.46) | data formatting | bytes 65536

commit v5 on v4

--- a/solution.py
+++ b/solution.py
@@ -9,7 +9,7 @@
 from jax.sharding import PartitionSpec as P
 
 MESH = pl.DeviceIdType.MESH
-GROUP = 48
+GROUP = 24
 FAR = 1 << 20
 
 
@@ -186,11 +186,10 @@
         lambda s: row_blocks[table_s[2, s]], lambda s: blk[table_s[1, s]], 3, 0)
 
     split(col_side, col_blocks, n_row)
-    total = jnp.zeros(run.shape[1:], f32)
-    for k in range(chunks):
-        chunk_copy(k).wait()
-        total = lax.fori_loop(k * per // group, (k + 1) * per // group, forward_group, total)
-        if k == (chunks - 1) // 2:
+
+    def forward_step(g, total):
+        @pl.when(g == chunks // 2)
+        def _():
             @pl.when(c < n_col - 1)
             def _():
                 pl.semaphore_wait(here, n_col - 1 - c)
@@ -198,6 +197,11 @@
             @pl.loop(c + 1, n_col)
             def _(p):
                 rs_copy(p, c).start()
+
+        chunk_copy(g).wait()
+        return forward_group(g, total)
+
+    lax.fori_loop(0, chunks, forward_step, jnp.zeros(run.shape[1:], f32))
 
     @pl.loop(0, n_col)
     def _(p):
@@ -224,20 +228,22 @@
             send_sem=f_send.at[d], recv_sem=f_recv.at[d],
             device_id=(r, to * 2 + core), device_id_type=MESH)
 
-    groups = slots // group
-    early = max(groups // 4, 1)
-    total = lax.fori_loop(0, early, backward_group, jnp.zeros(run.shape[1:], f32))
-    near_copy.wait()
-
-    @pl.loop(0, nz)
-    def _(p):
-        fwd[core, p] = fwd[core, p] + near[p]
-
-    @pl.loop(1, nz)
-    def _(d):
-        f_copy(d, True).start()
-
-    lax.fori_loop(early, groups, backward_group, total)
+    def backward_step(g, total):
+        @pl.when(g == chunks // 4)
+        def _():
+            near_copy.wait()
+
+            @pl.loop(0, nz)
+            def _(p):
+                fwd[core, p] = fwd[core, p] + near[p]
+
+            @pl.loop(1, nz)
+            def _(d):
+                f_copy(d, True).start()
+
+        return backward_group(g, total)
+
+    lax.fori_loop(0, chunks, backward_step, jnp.zeros(run.shape[1:], f32))
 
     @pl.loop(0, n_row)
     def _(p):

time: 20.2 us -> 20.4 us (level)
  no operation moved by 1% of the time
where the time goes in v5:
time: 20.4 us; the launch traced here: 20.1 us
  Pallas kernels  18.8 us (92%)
  local copies, waits for them, and re-layouts  1.38 us (7%)
    pallas_call x1, Pallas kernels, body(): pl.pallas_call(functools.partial(kernel, n_row, n_col, chunks, group), ou...  18.8 us
    unnamed x1, local copies, waits for them, and re-layouts  1.38 us

profile of v5, /device:TPU:0, one launch (start us, length us, event | category | flops | bytes accessed | tf_op | source)
XLA Modules:
  0.0 20.1 jit_solution(14537944612516513746)
XLA Ops:
  0.0 18.8 %shard_map.46 = f32[16,512]{1,0:T(8,128)} custom-call(bf16[16,512]{1,0:T(8,128)(2,1)} %vec_hbm.1, bf16[1,192,128,128]{3,2,1,0:T(8,128)(2,1)} %blk_hbm.1, s32[1,33]{1,0:T(1,128)} %ptr_hbm.1, s32[1,192]{1,0:T(1,128)} %col_hbm.1), custom_call_target="tpu_custom_call" | custom-call | flops 201326592 | bytes 6291456 | tf_op jit(solution)/shard_map/pallas_call | solution.py:310
  18.8 1.4 %copy.6 = f32[16,512]{1,0:T(8,128)} copy(f32[16,512]{1,0:T(8,128)} %shard_map.46) | data formatting | bytes 65536

commit v6 on v5

--- a/solution.py
+++ b/solution.py
@@ -9,7 +9,7 @@
 from jax.sharding import PartitionSpec as P
 
 MESH = pl.DeviceIdType.MESH
-GROUP = 24
+GROUP = 48
 FAR = 1 << 20
 
 
@@ -147,28 +147,20 @@
     def _(d):
         cs_copy(d, False).wait_recv()
 
-    def four_terms(sides, tiles, across):
-        if len(sides) != 4:
-            return [
-                lax.dot_general(x, t, (((1,), (across,)), ((), ())), preferred_element_type=f32)
-                for x, t in zip(sides, tiles)
-            ]
-        none = jnp.zeros_like(sides[0])
-        rows = [[sides[0], none], [sides[1], none], [none, sides[2]], [none, sides[3]]]
-        left = jnp.concatenate([jnp.concatenate(pair, 1) for pair in rows], 0)
-        places = ((0, 2), (1, 3)) if across else ((0, 1), (2, 3))
-        right = jnp.concatenate([jnp.concatenate([tiles[k] for k in pair], 1) for pair in places], 0)
+    def side_by_side(sides, tiles, across):
+        left = jnp.concatenate(sides, 0)
+        right = jnp.concatenate(tiles, 1 - across)
         out = lax.dot_general(left, right, (((1,), (across,)), ((), ())), preferred_element_type=f32)
-        m, n = none.shape
-        return [out[k * m:(k + 1) * m, (k % 2) * n:(k % 2 + 1) * n] for k in range(4)]
-
-    step = math.gcd(group, 4)
+        m, n = sides[0].shape
+        return [out[k * m:(k + 1) * m, k * n:(k + 1) * n] for k in range(len(sides))]
+
+    step = math.gcd(group, 2)
 
     def group_loop(side_of, tile_of, keep_row, across):
         def one_group(g, total):
             for j in range(0, group, step):
                 ids = [g * group + j + k for k in range(step)]
-                terms = four_terms([side_of(s) for s in ids], [tile_of(s) for s in ids], across)
+                terms = side_by_side([side_of(s) for s in ids], [tile_of(s) for s in ids], across)
                 for s, term in zip(ids, terms):
                     total = total * table_s[keep_row, s].astype(f32) + term
                     run[s] = total
@@ -229,7 +221,7 @@
             device_id=(r, to * 2 + core), device_id_type=MESH)
 
     def backward_step(g, total):
-        @pl.when(g == chunks // 4)
+        @pl.when(g == max(chunks // 4, 1))
         def _():
             near_copy.wait()
 

time: 20.4 us -> 20.2 us (level)
  no operation moved by 1% of the time
where the time goes in v6:
time: 20.2 us; the launch traced here: 20 us
  Pallas kernels  18.6 us (92%)
  local copies, waits for them, and re-layouts  1.38 us (7%)
    pallas_call x1, Pallas kernels, body(): pl.pallas_call(functools.partial(kernel, n_row, n_col, chunks, group), ou...  18.6 us
    unnamed x1, local copies, waits for them, and re-layouts  1.38 us

profile of v6, /device:TPU:0, one launch (start us, length us, event | category | flops | bytes accessed | tf_op | source)
XLA Modules:
  0.0 20.0 jit_solution(14252444509277271295)
XLA Ops:
  0.0 18.6 %shard_map.46 = f32[16,512]{1,0:T(8,128)} custom-call(bf16[16,512]{1,0:T(8,128)(2,1)} %vec_hbm.1, bf16[1,192,128,128]{3,2,1,0:T(8,128)(2,1)} %blk_hbm.1, s32[1,33]{1,0:T(1,128)} %ptr_hbm.1, s32[1,192]{1,0:T(1,128)} %col_hbm.1), custom_call_target="tpu_custom_call" | custom-call | flops 201326592 | bytes 6291456 | tf_op jit(solution)/shard_map/pallas_call | solution.py:302
  18.6 1.4 %copy.6 = f32[16,512]{1,0:T(8,128)} copy(f32[16,512]{1,0:T(8,128)} %shard_map.46) | data formatting | bytes 65536

commit v7 on v6

--- a/solution.py
+++ b/solution.py
@@ -60,13 +60,14 @@
     blk, ptr_s, col_s, ptr_v, col_v, table_v, table_s,
     row_side, col_side, row_blocks, col_blocks, run, fwd, bwd, near, fwd_in, bwd_in,
     here, vec_sem, blk_sem, idx_sem,
-    rs_send, rs_recv, cs_send, cs_recv, near_send, near_recv,
+    rs_send, rs_recv, relay_send, cs_send, cs_recv, near_send, near_recv,
     f_send, f_recv, b_send, b_recv,
 ):
     r = lax.axis_index("row")
     c = lax.axis_index("col")
     z, core = c // 2, c % 2
     nz = n_col // 2
+    sibling = z * 2 + 1 - core
     edge = blk.shape[1]
     seg = vec_hbm.shape[1] // edge
     slots = blk.shape[0]
@@ -120,6 +121,12 @@
             send_sem=rs_send.at[to], recv_sem=rs_recv.at[source],
             device_id=(r, to), device_id_type=MESH)
 
+    def relay(source):
+        return pltpu.make_async_remote_copy(
+            src_ref=row_side.at[source], dst_ref=row_side.at[source],
+            send_sem=relay_send.at[source], recv_sem=rs_recv.at[source],
+            device_id=(r, sibling), device_id_type=MESH)
+
     @pl.loop(1, n_row)
     def _(d):
         cs_copy(d, True).start()
@@ -127,7 +134,14 @@
     @pl.loop(0, c)
     def _(p):
         pl.semaphore_signal(here, inc=1, device_id=(r, p), device_id_type=MESH)
-        rs_copy(p, c).start()
+
+    @pl.loop(0, z)
+    def _(p):
+        rs_copy(p * 2 + core, c).start()
+
+    @pl.when(core == 1)
+    def _():
+        rs_copy(sibling, c).start()
 
     for k in range(chunks):
         chunk_copy(k).start()
@@ -186,9 +200,21 @@
             def _():
                 pl.semaphore_wait(here, n_col - 1 - c)
 
-            @pl.loop(c + 1, n_col)
+            @pl.loop(z + 1, nz)
             def _(p):
-                rs_copy(p, c).start()
+                rs_copy(p * 2 + core, c).start()
+
+            @pl.when(core == 0)
+            def _():
+                rs_copy(sibling, c).start()
+
+        @pl.when(g == chunks - 1)
+        def _():
+            @pl.loop(1, nz)
+            def _(d):
+                p = (z + nz - d) % nz * 2 + core
+                rs_copy(p, p).wait_recv()
+                relay(p).start()
 
         chunk_copy(g).wait()
         return forward_group(g, total)
@@ -206,9 +232,9 @@
         device_id=(r, z * 2 + 1 - core), device_id_type=MESH)
     near_copy.start()
 
-    @pl.loop(1, n_col)
-    def _(d):
-        p = (c + d) % n_col
+    @pl.loop(0, nz)
+    def _(d):
+        p = (z + d) % nz * 2 + 1 - core
         rs_copy(p, p).wait_recv()
 
     split(row_side, row_blocks, n_col)
@@ -279,9 +305,13 @@
         cs_copy(d, True).wait_send()
         b_copy(d, True).wait_send()
 
-    @pl.loop(1, n_col)
-    def _(d):
-        rs_copy((c + d) % n_col, c).wait_send()
+    rs_copy(sibling, c).wait_send()
+
+    @pl.loop(1, nz)
+    def _(d):
+        p = (z + d) % nz * 2 + core
+        rs_copy(p, c).wait_send()
+        relay(p).wait_send()
 
     @pl.loop(1, nz)
     def _(d):
@@ -323,7 +353,7 @@
             pltpu.VMEM((nz, seg, count, edge), f32),
             pltpu.VMEM((n_row, seg, count, edge), f32),
             pltpu.SemaphoreType.REGULAR, dma((2,)), dma((chunks,)), dma((4,)),
-            dma((n_col,)), dma((n_col,)), dma((n_row,)), dma((n_row,)), dma, dma,
+            dma((n_col,)), dma((n_col,)), dma((n_col,)), dma((n_row,)), dma((n_row,)), dma, dma,
             dma((nz,)), dma((nz,)), dma((n_row,)), dma((n_row,)),
         ],
         compiler_params=pltpu.CompilerParams(

time: 20.2 us -> 20.9 us (1.035)
  Pallas kernels: 18.6 us -> 19.3 us
    pallas_call x1, Pallas kernels: 18.6 us -> 19.3 us  [body(): pl.pallas_call(functools.partial(kernel, n_row, n_col, chunks, group), ou...]
where the time goes in v7:
time: 20.9 us; the launch traced here: 20.7 us
  Pallas kernels  19.3 us (92%)
  local copies, waits for them, and re-layouts  1.38 us (7%)
    pallas_call x1, Pallas kernels, body(): pl.pallas_call(functools.partial(kernel, n_row, n_col, chunks, group), ou...  19.3 us
    unnamed x1, local copies, waits for them, and re-layouts  1.38 us

profile of v7, /device:TPU:0, one launch (start us, length us, event | category | flops | bytes accessed | tf_op | source)
XLA Modules:
  0.0 20.7 jit_solution(2890877672214038921)
XLA Ops:
  0.0 19.3 %shard_map.46 = f32[16,512]{1,0:T(8,128)} custom-call(bf16[16,512]{1,0:T(8,128)(2,1)} %vec_hbm.1, bf16[1,192,128,128]{3,2,1,0:T(8,128)(2,1)} %blk_hbm.1, s32[1,33]{1,0:T(1,128)} %ptr_hbm.1, s32[1,192]{1,0:T(1,128)} %col_hbm.1), custom_call_target="tpu_custom_call" | custom-call | flops 201326592 | bytes 6291456 | tf_op jit(solution)/shard_map/pallas_call | solution.py:332
  19.3 1.4 %copy.6 = f32[16,512]{1,0:T(8,128)} copy(f32[16,512]{1,0:T(8,128)} %shard_map.46) | data formatting | bytes 65536
